TPU v7x, 32 devices: a whole 2x2x4 slice. The times are simulated.
32 devices in a mesh: lat: 4 (over z), lon: 8 (over y, x, core).
Axes of the slice: x: 2, y: 2, z: 4, core: 2. Of those that a mesh axis runs over, the one named last changes fastest.
Arguments:
- grid_input: bfloat16 [65536, 227], P(('lat', 'lon')), may hold values from -6 to 6
- mesh_input: bfloat16 [32768, 512], P(('lat', 'lon')), may hold values from -6 to 6
- cotangent: bfloat16 [32768, 512], P(('lat', 'lon')), may hold values from -0.078125 to 0.078125
- embed_weight: bfloat16 [227, 512], replicated, may hold values from -0.375 to 0.375
- enc_sender: bfloat16 [512, 512], replicated, may hold values from -0.25 to 0.25
- enc_receiver: bfloat16 [512, 512], replicated, may hold values from -0.25 to 0.25
- enc_update: bfloat16 [512, 512], replicated, may hold values from -0.25 to 0.25
- proc_sender: bfloat16 [512, 512], replicated, may hold values from -0.25 to 0.25
- proc_receiver: bfloat16 [512, 512], replicated, may hold values from -0.25 to 0.25
- proc_update: bfloat16 [512, 512], replicated, may hold values from -0.25 to 0.25
- grid_slots: int32 [16384], P(('lat', 'lon')), may hold values from 0 to 2047
- enc_edges: int32 [6, 32768], P(None, ('lat', 'lon')), may hold values from 0 to 2559, as said below
- mesh_slots: int32 [16384], P(('lat', 'lon')), may hold values from 0 to 1023
- mesh_edges: int32 [6, 32768], P(None, ('lat', 'lon')), may hold values from 0 to 1535, as said below
Outputs:
- mesh_out: bfloat16 [32768, 512], P(('lat', 'lon'))
- grad_embed: float32 [227, 512], replicated
- grad_enc_sender: float32 [512, 512], replicated
- grad_enc_receiver: float32 [512, 512], replicated
- grad_enc_update: float32 [512, 512], replicated
- grad_proc_sender: float32 [512, 512], replicated
- grad_proc_receiver: float32 [512, 512], replicated
- grad_proc_update: float32 [512, 512], replicated
Inputs may be any that keep to these rules, and one draw needn't show every extreme that they name: `enc_edges`: No entry names a neighbour beyond the first or last latitude band. `mesh_edges`: No entry names a neighbour beyond the first or last latitude band.
All inputs are finite; a program needn't handle non-finite values.
Results may differ from a plain program's by a relative error of at most 0.012.
Values may be sent and summed in bfloat16 or wider, within the bound.
A program may use at most 128 MiB of HBM per device.

v0:
```python
import jax
import jax.numpy as jnp
from jax import lax
from jax.sharding import PartitionSpec as P

lat_steps = (-1, -1, -1, 0, 0, 1, 1, 1)
lon_steps = (-1, 0, 1, -1, 1, -1, 0, 1)


def from_behind(block, axis, distance):
    devices = range(lax.axis_size(axis))
    route = [((i - distance) % len(devices), i) for i in devices]
    return lax.ppermute(block, axis, route)


def silu_slope(values):
    sigmoid = jax.nn.sigmoid(values)
    return sigmoid * (1.0 + values * (1.0 - sigmoid))


def transpose_dot(left, right):
    return lax.dot_general(
        left, right, (((0,), (0,)), ((), ())), preferred_element_type=jnp.float32
    )


def dot_transposed(left, right):
    return lax.dot_general(
        left, right, (((1,), (1,)), ((), ())), preferred_element_type=jnp.float32
    )


def code_move(outgoing, amount, returning):
    if returning:
        return from_behind(outgoing, ("lat", "lon"), amount)
    return from_behind(outgoing, ("lat", "lon"), amount)


def move_blocks(blocks, returning):
    lat_count = lax.axis_size("lat")
    lon_count = lax.axis_size("lon")
    lat_here = lax.axis_index("lat")
    lon_here = lax.axis_index("lon")
    pieces = []
    for code in range(8):
        lat_step = lat_steps[code]
        lon_step = lon_steps[code]
        outgoing = blocks[7 - code]
        straight = code_move(outgoing, -(lat_step * lon_count + lon_step), returning)
        if lon_step != 0:
            wrapped_block = code_move(
                outgoing, -(lat_step * lon_count + lon_step - lon_step * lon_count), returning
            )
            target_lon = lon_here + lon_step
            wrapped = (target_lon < 0) | (target_lon >= lon_count)
            received_block = jnp.where(wrapped, wrapped_block, straight)
        else:
            received_block = straight
        target_lat = lat_here + lat_step
        present = (target_lat >= 0) & (target_lat < lat_count)
        pieces.append(jnp.where(present, received_block, jnp.zeros_like(received_block)))
    result = jnp.stack(pieces)
    return result


def extend_rows(sender_rows, slot_rows):
    arrived = move_blocks(sender_rows[slot_rows], False)
    return jnp.concatenate([sender_rows, arrived.reshape(-1, sender_rows.shape[1])], axis=0)


def return_grads(sender_grad, slot_rows, own_count):
    feature_width = sender_grad.shape[1]
    outgoing = sender_grad[own_count:].reshape(slot_rows.shape + (feature_width,))
    returned = move_blocks(outgoing, True)
    remote_part = jax.ops.segment_sum(
        returned.reshape(-1, feature_width), slot_rows.reshape(-1), num_segments=own_count
    )
    return sender_grad[:own_count] + remote_part


def edge_sum(extended, receiver_rows, sources):
    before = extended[sources].astype(jnp.float32) + receiver_rows[None]
    return jnp.sum(jax.nn.silu(before), axis=0)


def edge_back(extended, receiver_rows, sources, grad_rows):
    before = extended[sources].astype(jnp.float32) + receiver_rows[None]
    edge_grad = grad_rows[None] * silu_slope(before)
    feature_width = edge_grad.shape[2]
    sender_grad = jax.ops.segment_sum(
        edge_grad.reshape(-1, feature_width), sources.reshape(-1), num_segments=extended.shape[0]
    )
    return (jnp.sum(edge_grad, axis=0), sender_grad)


def local(
    grid_input,
    mesh_input,
    cotangent,
    embed_weight,
    enc_sender,
    enc_receiver,
    enc_update,
    proc_sender,
    proc_receiver,
    proc_update,
    grid_slots,
    enc_edges,
    mesh_slots,
    mesh_edges,
):
    grid_count = grid_input.shape[0]
    mesh_count = mesh_input.shape[0]
    grid_table = grid_slots.reshape(8, -1)
    mesh_table = mesh_slots.reshape(8, -1)
    pre_grid = jnp.dot(grid_input, embed_weight, preferred_element_type=jnp.float32)
    grid_latent = jax.nn.silu(pre_grid).astype(jnp.bfloat16)
    enc_message = jnp.dot(grid_latent, enc_sender, preferred_element_type=jnp.float32).astype(
        jnp.bfloat16
    )
    enc_extended = extend_rows(enc_message, grid_table)
    enc_target = jnp.dot(mesh_input, enc_receiver, preferred_element_type=jnp.float32)
    enc_sum = edge_sum(enc_extended, enc_target, enc_edges).astype(jnp.bfloat16)
    mesh_mid = (
        mesh_input.astype(jnp.float32)
        + jnp.dot(enc_sum, enc_update, preferred_element_type=jnp.float32)
    ).astype(jnp.bfloat16)
    proc_message = jnp.dot(mesh_mid, proc_sender, preferred_element_type=jnp.float32).astype(
        jnp.bfloat16
    )
    proc_extended = extend_rows(proc_message, mesh_table)
    proc_target = jnp.dot(mesh_mid, proc_receiver, preferred_element_type=jnp.float32)
    proc_sum = edge_sum(proc_extended, proc_target, mesh_edges).astype(jnp.bfloat16)
    mesh_out = (
        mesh_mid.astype(jnp.float32)
        + jnp.dot(proc_sum, proc_update, preferred_element_type=jnp.float32)
    ).astype(jnp.bfloat16)
    grad_proc_update = transpose_dot(proc_sum, cotangent)
    grad_proc_sum = dot_transposed(cotangent, proc_update)
    proc_target_grad, proc_extended_grad = edge_back(
        proc_extended, proc_target, mesh_edges, grad_proc_sum
    )
    proc_message_grad = return_grads(proc_extended_grad, mesh_table, mesh_count).astype(
        jnp.bfloat16
    )
    proc_target_grad = proc_target_grad.astype(jnp.bfloat16)
    grad_proc_sender = transpose_dot(mesh_mid, proc_message_grad)
    grad_proc_receiver = transpose_dot(mesh_mid, proc_target_grad)
    mid_grad = (
        cotangent.astype(jnp.float32)
        + dot_transposed(proc_message_grad, proc_sender)
        + dot_transposed(proc_target_grad, proc_receiver)
    ).astype(jnp.bfloat16)
    grad_enc_update = transpose_dot(enc_sum, mid_grad)
    grad_enc_sum = dot_transposed(mid_grad, enc_update)
    enc_target_grad, enc_extended_grad = edge_back(
        enc_extended, enc_target, enc_edges, grad_enc_sum
    )
    enc_message_grad = return_grads(enc_extended_grad, grid_table, grid_count).astype(jnp.bfloat16)
    enc_target_grad = enc_target_grad.astype(jnp.bfloat16)
    grad_enc_receiver = transpose_dot(mesh_input, enc_target_grad)
    grad_enc_sender = transpose_dot(grid_latent, enc_message_grad)
    pre_grid_grad = (dot_transposed(enc_message_grad, enc_sender) * silu_slope(pre_grid)).astype(
        jnp.bfloat16
    )
    grad_embed = transpose_dot(grid_input, pre_grid_grad)
    (
        grad_embed,
        grad_enc_sender,
        grad_enc_receiver,
        grad_enc_update,
        grad_proc_sender,
        grad_proc_receiver,
        grad_proc_update,
    ) = lax.psum(
        (
            grad_embed,
            grad_enc_sender,
            grad_enc_receiver,
            grad_enc_update,
            grad_proc_sender,
            grad_proc_receiver,
            grad_proc_update,
        ),
        ("lat", "lon"),
    )
    return (
        mesh_out,
        grad_embed,
        grad_enc_sender,
        grad_enc_receiver,
        grad_enc_update,
        grad_proc_sender,
        grad_proc_receiver,
        grad_proc_update,
    )


def solution(mesh):
    placed = (
        P(("lat", "lon"), None),
        P(("lat", "lon"), None),
        P(("lat", "lon"), None),
        P(),
        P(),
        P(),
        P(),
        P(),
        P(),
        P(),
        P(("lat", "lon")),
        P(None, ("lat", "lon")),
        P(("lat", "lon")),
        P(None, ("lat", "lon")),
    )
    return jax.shard_map(
        local,
        mesh=mesh,
        in_specs=placed,
        out_specs=(P(("lat", "lon"), None), P(), P(), P(), P(), P(), P(), P()),
        check_vma=False,
    )
```

profile of v0, /device:TPU:0, one launch (start us, length us, event | category | flops | bytes accessed | tf_op | source)
XLA Modules:
  0.0 581.5 jit_solution(3304082588193844359)
XLA Ops:
  17.6 3.8 collective-permute-start.1
  24.4 3.5 collective-permute-start.5
  30.1 3.6 fusion.44
  35.4 5.4 collective-permute-done.2
  47.4 4.2 collective-permute-start.13
  52.5 3.8 collective-permute-done.11
  56.3 3.2 pad_maximum_fusion
  59.6 27.7 %gather_fusion.1 = bf16[6144,512]{1,0:T(8,128)(2,1)} fusion(bf16[2560,512]{1,0:T(8,128)(2,1)} %pad_maximum_fusion, s32[6144]{0:T(1024)S(1)} %get-tuple-element.69), kind=kCustom, calls=%fused_computation.1 | custom fusion | bytes 12607488 | tf_op jit(solution)/shard_map/gather | solution.py:82
  87.2 6.0 %multiply_reduce_fusion.3 = bf16[1024,512]{1,0:T(8,128)(2,1)S(1)} fusion(f32[1024,512]{1,0:T(8,128)S(1)} %fusion.42, bf16[6,1024,512]{2,1,0:T(8,128)(2,1)} %bitcast.149), kind=kLoop, calls=%fused_computation.30 | loop fusion | flops 21495808 | bytes 9437184 | tf_op jit(solution)/shard_map/reduce_sum | solution.py:83
  110.3 6.0 %collective-permute-done.16 = bf16[64,512]{1,0:T(8,128)(2,1)S(1)} collective-permute-done((bf16[64,512]{1,0:T(8,128)(2,1)S(1)}, bf16[64,512]{1,0:T(8,128)(2,1)S(1)}, u32[]{:S(2)}, u32[]{:S(2)}) %collective-permute-start.16) | collective-permute-done | bytes 65568 | tf_op jit(solution)/shard_map/ppermute | solution.py:13
  126.6 3.8 collective-permute-done.25
  131.9 25.4 %gather_fusion.3 = bf16[6144,512]{1,0:T(8,128)(2,1)} fusion(bf16[1536,512]{1,0:T(8,128)(2,1)S(1)} %pad_maximum_fusion.1, s32[6144]{0:T(1024)S(1)} %get-tuple-element.68), kind=kCustom, calls=%fused_computation.3 | custom fusion | bytes 12607488 | tf_op jit(solution)/shard_map/gather | solution.py:82
  157.3 9.7 %multiply_reduce_fusion.1 = (bf16[1024,512]{1,0:T(8,128)(2,1)S(1)}, bf16[1024,512]{1,0:T(8,128)(2,1)}, f32[6,1024,512]{2,1,0:T(8,128)S(1)}) fusion(f32[1024,512]{1,0:T(8,128)} %fusion.44, f32[1024,512]{1,0:T(8,128)} %fusion.43, bf16[6,1024,512]{2,1,0:T(8,128)(2,1)} %bitcast.153), kind=kLoop, calls=%fused_computation.27 | loop fusion | flops 39845888 | bytes 25165824 | tf_op jit(solution)/shard_map/reduce_sum | solution.py:93
  167.0 7.7 %fusion.11 = f32[6144,512]{1,0:T(8,128)} fusion(f32[6,1024,512]{2,1,0:T(8,128)S(1)} %get-tuple-element.35, f32[1024,512]{1,0:T(8,128)S(1)} %copy-done.5), kind=kLoop, calls=%fused_computation.25 | loop fusion | flops 25165824 | bytes 27262976 | tf_op jit(solution)/shard_map/mul | solution.py:88
  174.7 39.2 %scatter_custom_fusion = f32[1536,512]{1,0:T(8,128)} fusion(s32[6144]{0:T(1024)S(1)} %reshape.180, f32[6144,512]{1,0:T(8,128)} %fusion.11, f32[]{:T(128)} %constant.25.clone.1), kind=kCustom, calls=%fused_computation.43 | custom fusion | flops 3145728 | bytes 3146240 | tf_op jit(solution)/shard_map/scatter-add | solution.py:90
  227.9 5.2 collective-permute-done.29
  233.2 6.7 %collective-permute-done.30 = f32[64,512]{1,0:T(8,128)S(1)} collective-permute-done((f32[64,512]{1,0:T(8,128)S(1)}, f32[64,512]{1,0:T(8,128)S(1)}, u32[]{:S(2)}, u32[]{:S(2)}) %collective-permute-start.30) | collective-permute-done | bytes 131104 | tf_op jit(solution)/shard_map/ppermute | solution.py:13
  248.9 7.7 %collective-permute-done.39 = f32[64,512]{1,0:T(8,128)S(1)} collective-permute-done((f32[64,512]{1,0:T(8,128)S(1)}, f32[64,512]{1,0:T(8,128)S(1)}, u32[]{:S(2)}, u32[]{:S(2)}) %collective-permute-start.39) | collective-permute-done | bytes 131104 | tf_op jit(solution)/shard_map/ppermute | solution.py:13
  257.6 5.2 scatter_fusion
  269.1 6.3 %multiply_reduce_fusion = (bf16[1024,512]{1,0:T(8,128)(2,1)}, f32[6,1024,512]{2,1,0:T(8,128)S(1)}) fusion(f32[1024,512]{1,0:T(8,128)S(1)} %fusion.45, f32[1024,512]{1,0:T(8,128)S(1)} %copy-done.3, bf16[6,1024,512]{2,1,0:T(8,128)(2,1)S(1)} %bitcast.152), kind=kLoop, calls=%fused_computation.26 | loop fusion | flops 34078720 | bytes 24117248 | tf_op jit(solution)/shard_map/reduce_sum | solution.py:93
  275.3 7.7 %fusion.5 = f32[6144,512]{1,0:T(8,128)} fusion(f32[6,1024,512]{2,1,0:T(8,128)S(1)} %get-tuple-element.34, f32[1024,512]{1,0:T(8,128)S(1)} %fusion.45), kind=kLoop, calls=%fused_computation.17 | loop fusion | flops 25165824 | bytes 27262976 | tf_op jit(solution)/shard_map/mul | solution.py:88
  283.0 39.7 %scatter_custom_fusion.2 = f32[2560,512]{1,0:T(8,128)} fusion(s32[6144]{0:T(1024)S(1)} %reshape.196, f32[6144,512]{1,0:T(8,128)} %fusion.5, f32[]{:T(128)} %constant.25.clone.1), kind=kCustom, calls=%fused_computation.37 | custom fusion | flops 3145728 | bytes 5243392 | tf_op jit(solution)/shard_map/scatter-add | solution.py:90
  324.6 3.4 collective-permute-start.43
  328.0 4.4 collective-permute-start.45
  333.7 3.4 fusion.48
  347.1 6.6 %collective-permute-done.44 = f32[64,512]{1,0:T(8,128)S(1)} collective-permute-done((f32[64,512]{1,0:T(8,128)S(1)}, f32[64,512]{1,0:T(8,128)S(1)}, u32[]{:S(2)}, u32[]{:S(2)}) %collective-permute-start.44) | collective-permute-done | bytes 131104 | tf_op jit(solution)/shard_map/ppermute | solution.py:13
  361.0 4.0 collective-permute-start.55
  367.6 4.9 collective-permute-done.53
  372.6 7.7 %scatter_fusion.1 = f32[2048,512]{1,0:T(8,128)} fusion(f32[2048,512]{1,0:T(8,128)} %slice.219, s32[512]{0:T(512)S(1)} %copy-done.32, f32[512,512]{1,0:T(8,128)S(1)} %bitcast.157), kind=kCustom, calls=%fused_computation.7 | custom fusion | flops 262144 | bytes 3147776 | tf_op jit(solution)/shard_map/scatter-add | solution.py:75
  380.3 5.8 fusion.19
  386.1 6.9 %fusion.17 = f32[227,512]{1,0:T(8,128)} fusion(bf16[2048,227]{0,1:T(8,128)(2,1)S(1)} %copy-done, f32[2048,512]{1,0:T(8,128)} %copy-done.6, bf16[512,512]{1,0:T(8,128)(2,1)S(1)} %copy-done.34, f32[2048,512]{1,0:T(8,128)} %scatter_fusion.1), kind=kOutput, calls=%fused_computation.48 | convolution fusion | flops 1560281088 | bytes 10307584 | tf_op jit(solution)/shard_map/dot_general | solution.py:22
  397.2 164.9 %all-reduce.3.cloned.1.call-done = (f32[227,512]{1,0:T(8,128)}, f32[512,512]{1,0:T(8,128)}, f32[512,512]{0,1:T(8,128)}, f32[512,512]{1,0:T(8,128)}, f32[512,512]...) async-done(((f32[227,512]{1,0:T(8,128)}, f32[512,512]{1,0:T(8,128)}, f32[512,512]{0,1:T(8,128)}, f32[512,512]{1,0:T(8,128)}, f32[512,512]{1,0:T(8,128)}, ...) | async-done | bytes 6756368 | tf_op jit(solution)/shard_map/psum | solution.py:175
  (256 shorter events, 122.9 us)
Async XLA Ops:
  7.2 555.0 %all-reduce.3.cloned.1.call-start = ((), (), s32[]{:S(2)}) async-start(), calls=%async_computation | async-start | bytes 13533184 | tf_op jit(solution)/shard_map/psum | solution.py:175
  17.2 16.6 %collective-permute-start = (bf16[64,512]{1,0:T(8,128)(2,1)}, bf16[64,512]{1,0:T(8,128)(2,1)}, u32[]{:S(2)}, u32[]{:S(2)}) collective-permute-start(bf16[64,512]{1,0:T(8,128)(2,1)} %get-tuple-element.67), channel_id=1, source_target_pairs={{31,0},{0,1},{1,2},{2,3},{3,4},{4,5},{5,6},{6,7},{7,8},{8,9},{9,10... | collective-permute-start | bytes 196616 | tf_op jit(solution)/shard_map/ppermute | solution.py:13
  17.6 16.9 %collective-permute-start.1 = (bf16[64,512]{1,0:T(8,128)(2,1)}, bf16[64,512]{1,0:T(8,128)(2,1)}, u32[]{:S(2)}, u32[]{:S(2)}) collective-permute-start(bf16[64,512]{1,0:T(8,128)(2,1)} %get-tuple-element.67), channel_id=1, source_target_pairs={{23,0},{24,1},{25,2},{26,3},{27,4},{28,5},{29,6},{30,7},{31,8},{0,... | collective-permute-start | bytes 196616 | tf_op jit(solution)/shard_map/ppermute | solution.py:13
  21.4 21.1 %collective-permute-start.3 = (bf16[64,512]{1,0:T(8,128)(2,1)}, bf16[64,512]{1,0:T(8,128)(2,1)}, u32[]{:S(2)}, u32[]{:S(2)}) collective-permute-start(bf16[64,512]{1,0:T(8,128)(2,1)} %get-tuple-element.65), channel_id=1, source_target_pairs={{17,0},{18,1},{19,2},{20,3},{21,4},{22,5},{23,6},{24,7},{25,8},{26... | collective-permute-start | bytes 196616 | tf_op jit(solution)/shard_map/ppermute | solution.py:13
  24.3 21.2 %collective-permute-start.4 = (bf16[64,512]{1,0:T(8,128)(2,1)}, bf16[64,512]{1,0:T(8,128)(2,1)}, u32[]{:S(2)}, u32[]{:S(2)}) collective-permute-start(bf16[64,512]{1,0:T(8,128)(2,1)} %get-tuple-element.65), channel_id=1, source_target_pairs={{25,0},{26,1},{27,2},{28,3},{29,4},{30,5},{31,6},{0,7},{1,8},{2,9}... | collective-permute-start | bytes 196616 | tf_op jit(solution)/shard_map/ppermute | solution.py:13
  24.4 22.0 %collective-permute-start.5 = (bf16[64,512]{1,0:T(8,128)(2,1)S(1)}, bf16[64,512]{1,0:T(8,128)(2,1)}, u32[]{:S(2)}, u32[]{:S(2)}) collective-permute-start(bf16[64,512]{1,0:T(8,128)(2,1)S(1)} %get-tuple-element.64), channel_id=1, source_target_pairs={{7,0},{8,1},{9,2},{10,3},{11,4},{12,5},{13,6},{14,7},{15,8},{16,9}... | collective-permute-start | bytes 196616 | tf_op jit(solution)/shard_map/ppermute | solution.py:13
  33.8 12.7 %collective-permute-start.6 = (bf16[64,512]{1,0:T(8,128)(2,1)S(1)}, bf16[64,512]{1,0:T(8,128)(2,1)S(1)}, u32[]{:S(2)}, u32[]{:S(2)}) collective-permute-start(bf16[64,512]{1,0:T(8,128)(2,1)S(1)} %get-tuple-element.64), channel_id=1, source_target_pairs={{31,0},{0,1},{1,2},{2,3},{3,4},{4,5},{5,6},{6,7},{7,8},{8,9},{9,10... | collective-permute-start | bytes 196616 | tf_op jit(solution)/shard_map/ppermute | solution.py:13
  42.5 9.1 %collective-permute-start.8 = (bf16[64,512]{1,0:T(8,128)(2,1)S(1)}, bf16[64,512]{1,0:T(8,128)(2,1)S(1)}, u32[]{:S(2)}, u32[]{:S(2)}) collective-permute-start(bf16[64,512]{1,0:T(8,128)(2,1)S(1)} %get-tuple-element.63), channel_id=1, source_target_pairs={{1,0},{2,1},{3,2},{4,3},{5,4},{6,5},{7,6},{8,7},{9,8},{10,9},{11,1... | collective-permute-start | bytes 196616 | tf_op jit(solution)/shard_map/ppermute | solution.py:13
  46.4 9.9 %collective-permute-start.12 = (bf16[64,512]{1,0:T(8,128)(2,1)S(1)}, bf16[64,512]{1,0:T(8,128)(2,1)S(1)}, u32[]{:S(2)}, u32[]{:S(2)}) collective-permute-start(bf16[64,512]{1,0:T(8,128)(2,1)S(1)} %get-tuple-element.60), channel_id=1, source_target_pairs={{1,0},{2,1},{3,2},{4,3},{5,4},{6,5},{7,6},{8,7},{9,8},{10,9},{11,1... | collective-permute-start | bytes 196616 | tf_op jit(solution)/shard_map/ppermute | solution.py:13
  98.6 11.6 %collective-permute-start.14 = (bf16[64,512]{1,0:T(8,128)(2,1)S(1)}, bf16[64,512]{1,0:T(8,128)(2,1)S(1)}, u32[]{:S(2)}, u32[]{:S(2)}) collective-permute-start(bf16[64,512]{1,0:T(8,128)(2,1)S(1)} %get-tuple-element.59), channel_id=1, source_target_pairs={{31,0},{0,1},{1,2},{2,3},{3,4},{4,5},{5,6},{6,7},{7,8},{8,9},{9,10... | collective-permute-start | bytes 196616 | tf_op jit(solution)/shard_map/ppermute | solution.py:13
  98.7 11.5 %collective-permute-start.15 = (bf16[64,512]{1,0:T(8,128)(2,1)S(1)}, bf16[64,512]{1,0:T(8,128)(2,1)S(1)}, u32[]{:S(2)}, u32[]{:S(2)}) collective-permute-start(bf16[64,512]{1,0:T(8,128)(2,1)S(1)} %get-tuple-element.59), channel_id=1, source_target_pairs={{23,0},{24,1},{25,2},{26,3},{27,4},{28,5},{29,6},{30,7},{31,8},{0,... | collective-permute-start | bytes 196616 | tf_op jit(solution)/shard_map/ppermute | solution.py:13
  100.4 17.8 %collective-permute-start.17 = (bf16[64,512]{1,0:T(8,128)(2,1)S(1)}, bf16[64,512]{1,0:T(8,128)(2,1)S(1)}, u32[]{:S(2)}, u32[]{:S(2)}) collective-permute-start(bf16[64,512]{1,0:T(8,128)(2,1)S(1)} %get-tuple-element.57), channel_id=1, source_target_pairs={{17,0},{18,1},{19,2},{20,3},{21,4},{22,5},{23,6},{24,7},{25,8},{26... | collective-permute-start | bytes 196616 | tf_op jit(solution)/shard_map/ppermute | solution.py:13
  103.5 16.7 %collective-permute-start.18 = (bf16[64,512]{1,0:T(8,128)(2,1)S(1)}, bf16[64,512]{1,0:T(8,128)(2,1)S(1)}, u32[]{:S(2)}, u32[]{:S(2)}) collective-permute-start(bf16[64,512]{1,0:T(8,128)(2,1)S(1)} %get-tuple-element.57), channel_id=1, source_target_pairs={{25,0},{26,1},{27,2},{28,3},{29,4},{30,5},{31,6},{0,7},{1,8},{2,9}... | collective-permute-start | bytes 196616 | tf_op jit(solution)/shard_map/ppermute | solution.py:13
  104.9 15.4 %collective-permute-start.19 = (bf16[64,512]{1,0:T(8,128)(2,1)S(1)}, bf16[64,512]{1,0:T(8,128)(2,1)S(1)}, u32[]{:S(2)}, u32[]{:S(2)}) collective-permute-start(bf16[64,512]{1,0:T(8,128)(2,1)S(1)} %get-tuple-element.56), channel_id=1, source_target_pairs={{7,0},{8,1},{9,2},{10,3},{11,4},{12,5},{13,6},{14,7},{15,8},{16,9}... | collective-permute-start | bytes 196616 | tf_op jit(solution)/shard_map/ppermute | solution.py:13
  110.2 10.1 %collective-permute-start.20 = (bf16[64,512]{1,0:T(8,128)(2,1)S(1)}, bf16[64,512]{1,0:T(8,128)(2,1)S(1)}, u32[]{:S(2)}, u32[]{:S(2)}) collective-permute-start(bf16[64,512]{1,0:T(8,128)(2,1)S(1)} %get-tuple-element.56), channel_id=1, source_target_pairs={{31,0},{0,1},{1,2},{2,3},{3,4},{4,5},{5,6},{6,7},{7,8},{8,9},{9,10... | collective-permute-start | bytes 196616 | tf_op jit(solution)/shard_map/ppermute | solution.py:13
  120.3 10.2 %collective-permute-start.26 = (bf16[64,512]{1,0:T(8,128)(2,1)S(1)}, bf16[64,512]{1,0:T(8,128)(2,1)S(1)}, u32[]{:S(2)}, u32[]{:S(2)}) collective-permute-start(bf16[64,512]{1,0:T(8,128)(2,1)S(1)} %get-tuple-element.52), channel_id=1, source_target_pairs={{1,0},{2,1},{3,2},{4,3},{5,4},{6,5},{7,6},{8,7},{9,8},{10,9},{11,1... | collective-permute-start | bytes 196616 | tf_op jit(solution)/shard_map/ppermute | solution.py:13
  215.4 11.8 %collective-permute-start.28 = (f32[64,512]{1,0:T(8,128)S(1)}, f32[64,512]{1,0:T(8,128)S(1)}, u32[]{:S(2)}, u32[]{:S(2)}) collective-permute-start(f32[64,512]{1,0:T(8,128)S(1)} %get-tuple-element.51), channel_id=1, source_target_pairs={{31,0},{0,1},{1,2},{2,3},{3,4},{4,5},{5,6},{6,7},{7,8},{8,9},{9,10... | collective-permute-start | bytes 393224 | tf_op jit(solution)/shard_map/ppermute | solution.py:13
  215.4 17.7 %collective-permute-start.29 = (f32[64,512]{1,0:T(8,128)S(1)}, f32[64,512]{1,0:T(8,128)S(1)}, u32[]{:S(2)}, u32[]{:S(2)}) collective-permute-start(f32[64,512]{1,0:T(8,128)S(1)} %get-tuple-element.51), channel_id=1, source_target_pairs={{23,0},{24,1},{25,2},{26,3},{27,4},{28,5},{29,6},{30,7},{31,8},{0,... | collective-permute-start | bytes 393224 | tf_op jit(solution)/shard_map/ppermute | solution.py:13
  218.3 21.7 %collective-permute-start.31 = (f32[64,512]{1,0:T(8,128)S(1)}, f32[64,512]{1,0:T(8,128)S(1)}, u32[]{:S(2)}, u32[]{:S(2)}) collective-permute-start(f32[64,512]{1,0:T(8,128)S(1)} %get-tuple-element.49), channel_id=1, source_target_pairs={{17,0},{18,1},{19,2},{20,3},{21,4},{22,5},{23,6},{24,7},{25,8},{26... | collective-permute-start | bytes 393224 | tf_op jit(solution)/shard_map/ppermute | solution.py:13
  220.1 19.9 %collective-permute-start.32 = (f32[64,512]{1,0:T(8,128)S(1)}, f32[64,512]{1,0:T(8,128)S(1)}, u32[]{:S(2)}, u32[]{:S(2)}) collective-permute-start(f32[64,512]{1,0:T(8,128)S(1)} %get-tuple-element.49), channel_id=1, source_target_pairs={{25,0},{26,1},{27,2},{28,3},{29,4},{30,5},{31,6},{0,7},{1,8},{2,9}... | collective-permute-start | bytes 393224 | tf_op jit(solution)/shard_map/ppermute | solution.py:13
  225.1 16.2 %collective-permute-start.33 = (f32[64,512]{1,0:T(8,128)S(1)}, f32[64,512]{1,0:T(8,128)S(1)}, u32[]{:S(2)}, u32[]{:S(2)}) collective-permute-start(f32[64,512]{1,0:T(8,128)S(1)} %get-tuple-element.48), channel_id=1, source_target_pairs={{7,0},{8,1},{9,2},{10,3},{11,4},{12,5},{13,6},{14,7},{15,8},{16,9}... | collective-permute-start | bytes 393224 | tf_op jit(solution)/shard_map/ppermute | solution.py:13
  227.2 16.6 %collective-permute-start.34 = (f32[64,512]{1,0:T(8,128)S(1)}, f32[64,512]{1,0:T(8,128)S(1)}, u32[]{:S(2)}, u32[]{:S(2)}) collective-permute-start(f32[64,512]{1,0:T(8,128)S(1)} %get-tuple-element.48), channel_id=1, source_target_pairs={{31,0},{0,1},{1,2},{2,3},{3,4},{4,5},{5,6},{6,7},{7,8},{8,9},{9,10... | collective-permute-start | bytes 393224 | tf_op jit(solution)/shard_map/ppermute | solution.py:13
  243.7 12.8 %collective-permute-start.40 = (f32[64,512]{1,0:T(8,128)S(1)}, f32[64,512]{1,0:T(8,128)S(1)}, u32[]{:S(2)}, u32[]{:S(2)}) collective-permute-start(f32[64,512]{1,0:T(8,128)S(1)} %get-tuple-element.44), channel_id=1, source_target_pairs={{1,0},{2,1},{3,2},{4,3},{5,4},{6,5},{7,6},{8,7},{9,8},{10,9},{11,1... | collective-permute-start | bytes 393224 | tf_op jit(solution)/shard_map/ppermute | solution.py:13
  247.6 9.0 %collective-permute-start.41 = (f32[64,512]{1,0:T(8,128)S(1)}, f32[64,512]{1,0:T(8,128)S(1)}, u32[]{:S(2)}, u32[]{:S(2)}) collective-permute-start(f32[64,512]{1,0:T(8,128)S(1)} %get-tuple-element.44), channel_id=1, source_target_pairs={{9,0},{10,1},{11,2},{12,3},{13,4},{14,5},{15,6},{16,7},{17,8},{18,... | collective-permute-start | bytes 393224 | tf_op jit(solution)/shard_map/ppermute | solution.py:13
  324.2 21.2 %collective-permute-start.42 = (f32[64,512]{1,0:T(8,128)S(1)}, f32[64,512]{1,0:T(8,128)S(1)}, u32[]{:S(2)}, u32[]{:S(2)}) collective-permute-start(f32[64,512]{1,0:T(8,128)S(1)} %get-tuple-element.43), channel_id=1, source_target_pairs={{31,0},{0,1},{1,2},{2,3},{3,4},{4,5},{5,6},{6,7},{7,8},{8,9},{9,10... | collective-permute-start | bytes 393224 | tf_op jit(solution)/shard_map/ppermute | solution.py:13
  324.6 21.3 %collective-permute-start.43 = (f32[64,512]{1,0:T(8,128)S(1)}, f32[64,512]{1,0:T(8,128)S(1)}, u32[]{:S(2)}, u32[]{:S(2)}) collective-permute-start(f32[64,512]{1,0:T(8,128)S(1)} %get-tuple-element.43), channel_id=1, source_target_pairs={{23,0},{24,1},{25,2},{26,3},{27,4},{28,5},{29,6},{30,7},{31,8},{0,... | collective-permute-start | bytes 393224 | tf_op jit(solution)/shard_map/ppermute | solution.py:13
  328.0 28.2 %collective-permute-start.45 = (f32[64,512]{1,0:T(8,128)S(1)}, f32[64,512]{1,0:T(8,128)S(1)}, u32[]{:S(2)}, u32[]{:S(2)}) collective-permute-start(f32[64,512]{1,0:T(8,128)S(1)} %get-tuple-element.41), channel_id=1, source_target_pairs={{17,0},{18,1},{19,2},{20,3},{21,4},{22,5},{23,6},{24,7},{25,8},{26... | collective-permute-start | bytes 393224 | tf_op jit(solution)/shard_map/ppermute | solution.py:13
  332.4 26.5 %collective-permute-start.46 = (f32[64,512]{1,0:T(8,128)S(1)}, f32[64,512]{1,0:T(8,128)S(1)}, u32[]{:S(2)}, u32[]{:S(2)}) collective-permute-start(f32[64,512]{1,0:T(8,128)S(1)} %get-tuple-element.41), channel_id=1, source_target_pairs={{25,0},{26,1},{27,2},{28,3},{29,4},{30,5},{31,6},{0,7},{1,8},{2,9}... | collective-permute-start | bytes 393224 | tf_op jit(solution)/shard_map/ppermute | solution.py:13
  343.0 16.0 %collective-permute-start.47 = (f32[64,512]{1,0:T(8,128)S(1)}, f32[64,512]{1,0:T(8,128)S(1)}, u32[]{:S(2)}, u32[]{:S(2)}) collective-permute-start(f32[64,512]{1,0:T(8,128)S(1)} %get-tuple-element.40), channel_id=1, source_target_pairs={{7,0},{8,1},{9,2},{10,3},{11,4},{12,5},{13,6},{14,7},{15,8},{16,9}... | collective-permute-start | bytes 393224 | tf_op jit(solution)/shard_map/ppermute | solution.py:13
  345.4 13.7 %collective-permute-start.48 = (f32[64,512]{1,0:T(8,128)S(1)}, f32[64,512]{1,0:T(8,128)S(1)}, u32[]{:S(2)}, u32[]{:S(2)}) collective-permute-start(f32[64,512]{1,0:T(8,128)S(1)} %get-tuple-element.40), channel_id=1, source_target_pairs={{31,0},{0,1},{1,2},{2,3},{3,4},{4,5},{5,6},{6,7},{7,8},{8,9},{9,10... | collective-permute-start | bytes 393224 | tf_op jit(solution)/shard_map/ppermute | solution.py:13
  359.1 13.4 %collective-permute-start.54 = (f32[64,512]{1,0:T(8,128)S(1)}, f32[64,512]{1,0:T(8,128)S(1)}, u32[]{:S(2)}, u32[]{:S(2)}) collective-permute-start(f32[64,512]{1,0:T(8,128)S(1)} %get-tuple-element.36), channel_id=1, source_target_pairs={{1,0},{2,1},{3,2},{4,3},{5,4},{6,5},{7,6},{8,7},{9,8},{10,9},{11,1... | collective-permute-start | bytes 393224 | tf_op jit(solution)/shard_map/ppermute | solution.py:13
  361.0 11.5 %collective-permute-start.55 = (f32[64,512]{1,0:T(8,128)S(1)}, f32[64,512]{1,0:T(8,128)S(1)}, u32[]{:S(2)}, u32[]{:S(2)}) collective-permute-start(f32[64,512]{1,0:T(8,128)S(1)} %get-tuple-element.36), channel_id=1, source_target_pairs={{9,0},{10,1},{11,2},{12,3},{13,4},{14,5},{15,6},{16,7},{17,8},{18,... | collective-permute-start | bytes 393224 | tf_op jit(solution)/shard_map/ppermute | solution.py:13
  (65 other events, 671.1 us)
Sparse Core Ops, SparseCore 0:
  393.1 168.9 all-reduce.2
where the time goes:
time: 591 us; the launch traced here: 581 us
  waiting for transfers between devices  221 us (37%)
  other arithmetic  137 us (23%)
  local copies, waits for them, and re-layouts  84.9 us (14%)
  starting transfers between devices  79.1 us (13%)
  matrix products  44.2 us (7%)
  between operations  15.4 us (3%)
    psum x1, waiting for transfers between devices, local(): lax.psum((grad_embed, grad_enc_sender, grad_enc_receiver, grad_enc_update...  165 us
    ppermute x56, starting transfers between devices, from_behind(): return lax.ppermute(block, axis, route)  79 us
    scatter-add x2, other arithmetic, edge_back(): jax.ops.segment_sum(edge_grad.reshape(-1, feature_width), sources.reshape...  78.9 us
    ppermute x56, waiting for transfers between devices, from_behind(): return lax.ppermute(block, axis, route)  56.2 us
    gather x2, local copies, waits for them, and re-layouts, edge_sum(): before = extended[sources].astype(jnp.float32) + receiver_rows[None]  53.1 us
    dot_general x7, matrix products, transpose_dot(): lax.dot_general(left, right, (((0,), (0,)), ((), ())), preferred_element_...  23 us
    unnamed x85, local copies, waits for them, and re-layouts  16.5 us
    reduce_sum x2, other arithmetic, edge_back(): return (jnp.sum(edge_grad, axis=0), sender_grad)  16 us
  transfers between devices with their start and end apart: 57, of which 13 were waited for; matrix products, arithmetic and copies ran while one was open for 5% of the time, Pallas kernels for 0%

commit v1 on v0

v1 whole, which is shorter than its diff:
```python
import jax
import jax.numpy as jnp
from jax import lax
from jax.experimental import pallas as pl
from jax.experimental.pallas import tpu as pltpu
from jax.sharding import PartitionSpec as P

lat_steps = (-1, -1, -1, 0, 0, 1, 1, 1)
lon_steps = (-1, 0, 1, -1, 1, -1, 0, 1)
MESH = pl.DeviceIdType.MESH
BLOCK = 512


def neighbour(code):
    lat_count = lax.axis_size("lat")
    lon_count = lax.axis_size("lon")
    lat = lax.axis_index("lat") + lat_steps[code]
    lon = lax.rem(lax.axis_index("lon") + lon_steps[code] + lon_count, lon_count)
    return (lat, lon), (lat >= 0) & (lat < lat_count)


def greet():
    barrier = pltpu.get_barrier_semaphore()
    for code in range(8):
        device, present = neighbour(code)

        @pl.when(present)
        def _():
            pl.semaphore_signal(barrier, inc=1, device_id=device, device_id_type=MESH)


def await_greetings():
    lat = lax.axis_index("lat")
    last = lax.axis_size("lat") - 1
    peers = 2 + 3 * jnp.minimum(lat, 1) + 3 * jnp.minimum(last - lat, 1)
    pl.semaphore_wait(pltpu.get_barrier_semaphore(), peers)


def block_copy(code, land, outgoing, arrived, send_sem, recv_sem):
    cap = outgoing.shape[0] // 8
    device, present = neighbour(code)
    copy = pltpu.make_async_remote_copy(
        src_ref=outgoing.at[pl.ds(code * cap, cap)],
        dst_ref=arrived.at[pl.ds(land * cap, cap)],
        send_sem=send_sem.at[code],
        recv_sem=recv_sem.at[land],
        device_id=device,
        device_id_type=MESH,
    )
    return copy, present


def send_blocks(outgoing, arrived, send_sem, recv_sem):
    cap = outgoing.shape[0] // 8
    for code in range(8):
        copy, present = block_copy(code, 7 - code, outgoing, arrived, send_sem, recv_sem)

        @pl.when(present)
        def _():
            copy.start()

        @pl.when(jnp.logical_not(present))
        def _():
            arrived[pl.ds(code * cap, cap)] = jnp.zeros((cap, arrived.shape[1]), arrived.dtype)


def await_blocks(outgoing, arrived, send_sem, recv_sem):
    for code in range(8):
        copy, present = block_copy(code, code, outgoing, arrived, send_sem, recv_sem)

        @pl.when(present)
        def _():
            copy.wait_send()
            copy.wait_recv()


def pick(column, width, first=0):
    lanes = lax.broadcasted_iota(jnp.int32, (column.shape[0], width), 1) + first
    return jnp.where(column == lanes, 1.0, 0.0).astype(jnp.bfloat16)


def place(row, height, first):
    sublanes = lax.broadcasted_iota(jnp.int32, (height, row.shape[1]), 0) + first
    return jnp.where(row == sublanes, 1.0, 0.0).astype(jnp.bfloat16)


def matmul(left, right):
    return jnp.dot(left, right, preferred_element_type=jnp.float32)


def forward_kernel(
    rows, slots, edges, target, sums, slope, outgoing, arrived, send_sem, recv_sem
):
    own = rows.shape[0]
    fan, count, width = slope.shape
    slot_count = outgoing.shape[0]
    greet()
    outgoing[...] = matmul(pick(slots[...], own), rows[...]).astype(jnp.bfloat16)
    await_greetings()
    send_blocks(outgoing, arrived, send_sem, recv_sem)

    @pl.loop(0, count // BLOCK)
    def _(step):
        here = pl.ds(pl.multiple_of(step * BLOCK, BLOCK), BLOCK)
        for k in range(fan):
            slope[k, here] = matmul(pick(edges[here, k : k + 1], own), rows[...]).astype(
                jnp.bfloat16
            )

    await_blocks(outgoing, arrived, send_sem, recv_sem)
    half = BLOCK // 2

    @pl.loop(0, count // half)
    def _(step):
        here = pl.ds(pl.multiple_of(step * half, half), half)
        total = jnp.zeros((half, width), jnp.float32)
        for k in range(fan):
            far = matmul(pick(edges[here, k : k + 1], slot_count, own), arrived[...])
            before = slope[k, here].astype(jnp.float32) + far + target[here]
            sigmoid = 0.5 * jnp.tanh(0.5 * before) + 0.5
            total = total + before * sigmoid
            slope[k, here] = (sigmoid * (1.0 + before * (1.0 - sigmoid))).astype(jnp.bfloat16)
        sums[here] = total.astype(jnp.bfloat16)


def backward_kernel(
    slope, grad, edges, slots, target_grad, message_grad, edge_grad, local, outgoing, arrived, send_sem, recv_sem
):
    own = message_grad.shape[0]
    fan, count, width = slope.shape
    slot_count = outgoing.shape[0]
    half = BLOCK // 2
    greet()

    @pl.loop(0, count // half)
    def _(step):
        first = pl.multiple_of(step * half, half)
        here = pl.ds(first, half)
        total = jnp.zeros((half, width), jnp.float32)
        for k in range(fan):
            one = grad[here] * slope[k, here].astype(jnp.float32)
            total = total + one
            edge_grad[pl.ds(pl.multiple_of(k * count + first, half), half)] = one.astype(jnp.bfloat16)
        target_grad[here] = total.astype(jnp.bfloat16)

    outgoing[...] = matmul(place(edges[...], slot_count, own), edge_grad[...]).astype(jnp.bfloat16)
    await_greetings()
    send_blocks(outgoing, arrived, send_sem, recv_sem)

    @pl.loop(0, own // BLOCK)
    def _(step):
        first = pl.multiple_of(step * BLOCK, BLOCK)
        local[pl.ds(first, BLOCK)] = matmul(place(edges[...], BLOCK, first), edge_grad[...])

    await_blocks(outgoing, arrived, send_sem, recv_sem)

    @pl.loop(0, own // BLOCK)
    def _(step):
        first = pl.multiple_of(step * BLOCK, BLOCK)
        here = pl.ds(first, BLOCK)
        far = matmul(place(slots[...], BLOCK, first), arrived[...])
        message_grad[here] = (local[here] + far).astype(jnp.bfloat16)


def halo_scratch(slot_count, width):
    return [
        pltpu.VMEM((slot_count, width), jnp.bfloat16),
        pltpu.VMEM((slot_count, width), jnp.bfloat16),
        pltpu.SemaphoreType.DMA((8,)),
        pltpu.SemaphoreType.DMA((8,)),
    ]


def edge_forward(rows, slots, edges, target, number):
    own, width = rows.shape
    fan, count = edges.shape
    slot_count = slots.shape[0]
    vmem = pl.BlockSpec(memory_space=pltpu.VMEM)
    return pl.pallas_call(
        forward_kernel,
        out_shape=(
            jax.ShapeDtypeStruct((count, width), jnp.bfloat16),
            jax.ShapeDtypeStruct((fan, count, width), jnp.bfloat16),
        ),
        in_specs=[vmem] * 4,
        out_specs=(vmem, vmem),
        scratch_shapes=halo_scratch(slot_count, width),
        compiler_params=pltpu.CompilerParams(
            collective_id=number, has_side_effects=True, vmem_limit_bytes=50 * 2**20
        ),
        cost_estimate=pl.CostEstimate(
            flops=2 * fan * count * (own + slot_count) * width,
            bytes_accessed=12 * count * width,
            transcendentals=fan * count * width,
        ),
    )(rows, slots.reshape(-1, 1), edges.T, target)


def edge_backward(slope, grad, edges, slots, own, number):
    fan, count, width = slope.shape
    slot_count = slots.shape[0]
    vmem = pl.BlockSpec(memory_space=pltpu.VMEM)
    return pl.pallas_call(
        backward_kernel,
        out_shape=(
            jax.ShapeDtypeStruct((count, width), jnp.bfloat16),
            jax.ShapeDtypeStruct((own, width), jnp.bfloat16),
        ),
        in_specs=[vmem] * 4,
        out_specs=(vmem, vmem),
        scratch_shapes=[
            pltpu.VMEM((fan * count, width), jnp.bfloat16),
            pltpu.VMEM((own, width), jnp.float32),
        ]
        + halo_scratch(slot_count, width),
        compiler_params=pltpu.CompilerParams(
            collective_id=number, has_side_effects=True, vmem_limit_bytes=50 * 2**20
        ),
        cost_estimate=pl.CostEstimate(
            flops=2 * fan * count * (own + slot_count) * width,
            bytes_accessed=12 * count * width,
            transcendentals=0,
        ),
    )(slope, grad, edges.reshape(1, -1), slots.reshape(1, -1))


def silu_slope(values):
    sigmoid = jax.nn.sigmoid(values)
    return sigmoid * (1.0 + values * (1.0 - sigmoid))


def transpose_dot(left, right):
    return lax.dot_general(
        left, right, (((0,), (0,)), ((), ())), preferred_element_type=jnp.float32
    )


def dot_transposed(left, right):
    return lax.dot_general(
        left, right, (((1,), (1,)), ((), ())), preferred_element_type=jnp.float32
    )


def local(
    grid_input,
    mesh_input,
    cotangent,
    embed_weight,
    enc_sender,
    enc_receiver,
    enc_update,
    proc_sender,
    proc_receiver,
    proc_update,
    grid_slots,
    enc_edges,
    mesh_slots,
    mesh_edges,
):
    grid_count = grid_input.shape[0]
    mesh_count = mesh_input.shape[0]
    pre_grid = jnp.dot(grid_input, embed_weight, preferred_element_type=jnp.float32)
    grid_latent = jax.nn.silu(pre_grid).astype(jnp.bfloat16)
    enc_message = jnp.dot(grid_latent, enc_sender, preferred_element_type=jnp.float32).astype(
        jnp.bfloat16
    )
    enc_target = jnp.dot(mesh_input, enc_receiver, preferred_element_type=jnp.float32)
    enc_sum, enc_slope = edge_forward(enc_message, grid_slots, enc_edges, enc_target, 0)
    mesh_mid = (
        mesh_input.astype(jnp.float32)
        + jnp.dot(enc_sum, enc_update, preferred_element_type=jnp.float32)
    ).astype(jnp.bfloat16)
    proc_message = jnp.dot(mesh_mid, proc_sender, preferred_element_type=jnp.float32).astype(
        jnp.bfloat16
    )
    proc_target = jnp.dot(mesh_mid, proc_receiver, preferred_element_type=jnp.float32)
    proc_sum, proc_slope = edge_forward(proc_message, mesh_slots, mesh_edges, proc_target, 1)
    mesh_out = (
        mesh_mid.astype(jnp.float32)
        + jnp.dot(proc_sum, proc_update, preferred_element_type=jnp.float32)
    ).astype(jnp.bfloat16)
    grad_proc_update = transpose_dot(proc_sum, cotangent)
    grad_proc_sum = dot_transposed(cotangent, proc_update)
    proc_target_grad, proc_message_grad = edge_backward(
        proc_slope, grad_proc_sum, mesh_edges, mesh_slots, mesh_count, 2
    )
    grad_proc_sender = transpose_dot(mesh_mid, proc_message_grad)
    grad_proc_receiver = transpose_dot(mesh_mid, proc_target_grad)
    mid_grad = (
        cotangent.astype(jnp.float32)
        + dot_transposed(proc_message_grad, proc_sender)
        + dot_transposed(proc_target_grad, proc_receiver)
    ).astype(jnp.bfloat16)
    grad_enc_update = transpose_dot(enc_sum, mid_grad)
    grad_enc_sum = dot_transposed(mid_grad, enc_update)
    early = lax.psum(
        jnp.stack([grad_proc_update, grad_proc_sender, grad_proc_receiver, grad_enc_update]).astype(
            jnp.bfloat16
        ),
        ("lat", "lon"),
    )
    enc_target_grad, enc_message_grad = edge_backward(
        enc_slope, grad_enc_sum, enc_edges, grid_slots, grid_count, 3
    )
    grad_enc_receiver = transpose_dot(mesh_input, enc_target_grad)
    grad_enc_sender = transpose_dot(grid_latent, enc_message_grad)
    pre_grid_grad = (dot_transposed(enc_message_grad, enc_sender) * silu_slope(pre_grid)).astype(
        jnp.bfloat16
    )
    grad_embed = transpose_dot(grid_input, pre_grid_grad)
    late = jnp.concatenate([grad_enc_sender, grad_enc_receiver, grad_embed]).astype(jnp.bfloat16)
    late, early = lax.optimization_barrier((late, early))
    late = lax.psum(late, ("lat", "lon")).astype(jnp.float32)
    early = early.astype(jnp.float32)
    latent_width = enc_sender.shape[0]
    grad_enc_sender = late[:latent_width]
    grad_enc_receiver = late[latent_width : 2 * latent_width]
    grad_embed = late[2 * latent_width :]
    grad_proc_update, grad_proc_sender, grad_proc_receiver, grad_enc_update = early
    return (
        mesh_out,
        grad_embed,
        grad_enc_sender,
        grad_enc_receiver,
        grad_enc_update,
        grad_proc_sender,
        grad_proc_receiver,
        grad_proc_update,
    )


def solution(mesh):
    placed = (
        P(("lat", "lon"), None),
        P(("lat", "lon"), None),
        P(("lat", "lon"), None),
        P(),
        P(),
        P(),
        P(),
        P(),
        P(),
        P(),
        P(("lat", "lon")),
        P(None, ("lat", "lon")),
        P(("lat", "lon")),
        P(None, ("lat", "lon")),
    )
    return jax.shard_map(
        local,
        mesh=mesh,
        in_specs=placed,
        out_specs=(P(("lat", "lon"), None), P(), P(), P(), P(), P(), P(), P()),
        check_vma=False,
    )
```

time: 591 us -> 388 us (0.66); the launches traced: 581 us -> 384 us
  other arithmetic: 137 us -> 4.73 us
  Pallas kernels: 0 us -> 94.2 us
  starting transfers between devices: 79.1 us -> 0.08 us
  local copies, waits for them, and re-layouts: 84.9 us -> 12.2 us
  matrix products: 44.2 us -> 33.5 us
    pallas_call x0 -> x4, Pallas kernels: none -> 94.2 us  [the longest x2 52.5 us: edge_forward(): pl.pallas_call(forward_kernel, out_shape=(jax.ShapeDtypeStruct((count, wi...]
    scatter-add x4 -> x0, other arithmetic: 91.8 us -> none  [the longest x2 78.9 us: edge_back(): jax.ops.segment_sum(edge_grad.reshape(-1, feature_width), sources.reshape...]
    ppermute x56 -> x0, starting transfers between devices: 79 us -> none  [from_behind(): return lax.ppermute(block, axis, route)]
    psum x1 -> x2, waiting for transfers between devices: 165 us -> 225 us  [the longest x1 131 us: local(): late = lax.psum(late, ('lat', 'lon')).astype(jnp.float32)]
    gather x4 -> x0, local copies, waits for them, and re-layouts: 58.3 us -> none  [the longest x2 53.1 us: edge_sum(): before = extended[sources].astype(jnp.float32) + receiver_rows[None]]
    ppermute x56 -> x0, waiting for transfers between devices: 56.2 us -> none  [from_behind(): return lax.ppermute(block, axis, route)]
    reduce_sum x3 -> x0, other arithmetic: 21.9 us -> none  [the longest x2 16 us: edge_back(): return (jnp.sum(edge_grad, axis=0), sender_grad)]
    mul x2 -> x0, other arithmetic: 15.3 us -> none  [edge_back(): edge_grad = grad_rows[None] * silu_slope(before)]
  transfers between devices with their start and end apart: 57 -> 2, of which waited for: 13 -> 2; matrix products, arithmetic and copies ran while one was open for 5% -> 5% of each run, Pallas kernels for 0% -> 6%
where the time goes in v1:
time: 388 us; the launch traced here: 384 us
  waiting for transfers between devices  225 us (58%)
  Pallas kernels  94.2 us (24%)
  matrix products  33.5 us (9%)
  between operations  14.7 us (4%)
  local copies, waits for them, and re-layouts  12.2 us (3%)
  other arithmetic  4.73 us (1%)
    psum x1, waiting for transfers between devices, local(): late = lax.psum(late, ('lat', 'lon')).astype(jnp.float32)  131 us
    psum x1, waiting for transfers between devices, local(): lax.psum(jnp.stack([grad_proc_update, grad_proc_sender, grad_proc_receive...  94.2 us
    pallas_call x2, Pallas kernels, edge_forward(): pl.pallas_call(forward_kernel, out_shape=(jax.ShapeDtypeStruct((count, wi...  52.5 us
    pallas_call x2, Pallas kernels, edge_backward(): pl.pallas_call(backward_kernel, out_shape=(jax.ShapeDtypeStruct((count, w...  41.7 us
    dot_general x7, matrix products, transpose_dot(): lax.dot_general(left, right, (((0,), (0,)), ((), ())), preferred_element_...  11.6 us
  transfers between devices with their start and end apart: 2, of which 2 were waited for; matrix products, arithmetic and copies ran while one was open for 5% of the time, Pallas kernels for 6%

profile of v1, /device:TPU:0, one launch (start us, length us, event | category | flops | bytes accessed | tf_op | source)
XLA Modules:
  0.0 384.4 jit_solution(3812587563617026719)
XLA Ops:
  7.2 1.0 copy.24
  8.3 0.8 copy.25.slots
  9.1 4.2 %multiply_convert_fusion.1 = (bf16[2048,512]{1,0:T(8,128)(2,1)S(1)}, f32[2048,512]{1,0:T(8,128)}) fusion(bf16[2048,227]{0,1:T(8,128)(2,1)S(1)} %copy-done, bf16[227,512]{1,0:T(8,128)(2,1)} %param.17), kind=kOutput, calls=%fused_computation.1 | convolution fusion | flops 481296384 | bytes 7453696 | tf_op jit(solution)/shard_map/dot_general | solution.py:262
  13.4 1.2 convolution_convert_fusion.rows
  15.5 2.1 fusion.10.target
  17.6 30.4 %shard_map.197 = (bf16[1024,512]{1,0:T(8,128)(2,1)S(1)}, bf16[6,1024,512]{2,1,0:T(8,128)(2,1)}) custom-call(bf16[2048,512]{1,0:T(8,128)(2,1)S(1)} %convolution_convert_fusion.rows, s32[512,1]{1,0:T(8,128)S(1)} %copy.25.slots, s32[1024,6]{1,0:T(8,128)S(1)} %bitcast.69, f32[1024,512]{1,0:T(8,128)} %fusion.10.target), custom_call_target="tpu_custom_call" | custom-call | flops 16106127360 | bytes 6291456 | tf_op jit(solution)/shard_map/pallas_call | solution.py:179
  48.0 0.7 add_convert_fusion.2
  49.0 2.0 fusion.11.target
  51.0 1.7 convolution_convert_fusion.1.rows
  53.2 3.6 fusion.12.grad
  56.7 22.1 %shard_map.198 = (bf16[1024,512]{1,0:T(8,128)(2,1)S(1)}, bf16[6,1024,512]{2,1,0:T(8,128)(2,1)}) custom-call(bf16[1024,512]{1,0:T(8,128)(2,1)S(1)} %copy-done.5, s32[512,1]{1,0:T(8,128)S(1)} %copy.27.slots, s32[1024,6]{1,0:T(8,128)S(1)} %bitcast.70, f32[1024,512]{1,0:T(8,128)} %fusion.11.target), custom_call_target="tpu_custom_call" | custom-call | flops 9663676416 | bytes 6291456 | tf_op jit(solution)/shard_map/pallas_call | solution.py:179
  78.8 17.0 %shard_map.199 = (bf16[1024,512]{1,0:T(8,128)(2,1)S(1)}, bf16[1024,512]{1,0:T(8,128)(2,1)S(1)}) custom-call(bf16[6,1024,512]{2,1,0:T(8,128)(2,1)} %get-tuple-element.21.slope, f32[1024,512]{1,0:T(8,128)} %fusion.12.grad, s32[1,6144]{1,0:T(1,128)S(1)} %bitcast.71, s32[1,512]{1,0:T(1,128)S(1)} %bitcast.74), custom_call_target="tpu_custom_call" | custom-call | flops 9663676416 | bytes 6291456 | tf_op jit(solution)/shard_map/pallas_call | solution.py:203
  95.9 0.7 fusion.13
  97.1 0.7 fusion.3
  97.9 0.7 fusion.4
  99.2 0.7 add_convert_fusion
  99.9 0.7 fusion.5
  100.7 0.7 fusion.2
  101.4 1.6 pad_maximum_fusion
  103.2 0.9 copy-done.20
  104.1 2.1 fusion.14.grad
  106.3 24.7 %shard_map.200 = (bf16[1024,512]{1,0:T(8,128)(2,1)S(1)}, bf16[2048,512]{1,0:T(8,128)(2,1)S(1)}) custom-call(bf16[6,1024,512]{2,1,0:T(8,128)(2,1)} %get-tuple-element.20.slope, f32[1024,512]{1,0:T(8,128)} %fusion.14.grad, s32[1,6144]{1,0:T(1,128)S(1)} %bitcast.72, s32[1,512]{1,0:T(1,128)S(1)} %bitcast.76), custom_call_target="tpu_custom_call" | custom-call | flops 16106127360 | bytes 6291456 | tf_op jit(solution)/shard_map/pallas_call | solution.py:203
  131.0 2.1 convolution_convert_fusion.2
  133.0 1.6 fusion.1
  134.6 5.0 %fusion.7 = bf16[227,512]{1,0:T(8,128)(2,1)S(1)} fusion(bf16[2048,227]{0,1:T(8,128)(2,1)S(1)} %copy-done, f32[2048,512]{1,0:T(8,128)} %get-tuple-element.35, bf16[2048,512]{1,0:T(8,128)(2,1)S(1)} %get-tuple-element.24, bf16[512,512]{1,0:T(8,128)(2,1)} %param.18), kind=kOutput, calls=%fused_computation.23 | convolution fusion | flops 1559348736 | bytes 7977984 | tf_op jit(solution)/shard_map/dot_general | solution.py:233
  139.7 2.5 pad_maximum_fusion.1
  142.2 94.2 %all-reduce.3.cloned.1.call-done = bf16[4,512,512]{2,1,0:T(8,128)(2,1)} async-done(((bf16[4,512,512]{2,1,0:T(8,128)(2,1)}), bf16[4,512,512]{2,1,0:T(8,128)(2,1)}) %all-reduce.3.cloned.1.call-update) | async-done | bytes 2097168 | tf_op jit(solution)/shard_map/psum | solution.py:296
  236.4 2.9 add_convert_fusion.1
  239.8 2.1 slice_bitcast_fusion
  241.9 130.8 %all-reduce.5.cloned.1.call-done = bf16[1251,512]{1,0:T(8,128)(2,1)} async-done(((bf16[1251,512]{1,0:T(8,128)(2,1)}), bf16[1251,512]{1,0:T(8,128)(2,1)}) %all-reduce.5.cloned.1.call-update) | async-done | bytes 1281040 | tf_op jit(solution)/shard_map/psum | solution.py:313
  372.7 2.8 fusion.9
  375.5 1.8 slice.12
  (56 shorter events, 3.5 us)
Async XLA Ops:
  7.2 2.0 copy-start
  7.2 229.2 %all-reduce.3.cloned.1.call-start = ((), (), s32[]{:S(2)}) async-start(), calls=%async_computation | async-start | bytes 4194304 | tf_op jit(solution)/shard_map/psum | solution.py:296
  9.1 4.2 %copy-start.23 = (bf16[512,512]{1,0:T(8,128)(2,1)S(1)}, bf16[512,512]{1,0:T(8,128)(2,1)}, u32[]{:S(2)}) copy-start(bf16[512,512]{1,0:T(8,128)(2,1)} %param.18) | copy-start | bytes 1572868
  13.4 1.3 copy-start.8
  13.4 2.0 copy-start.12
  13.4 2.1 copy-start.17
  17.6 30.4 %copy-start.19 = (bf16[512,512]{1,0:T(8,128)(2,1)S(1)}, bf16[512,512]{1,0:T(8,128)(2,1)}, u32[]{:S(2)}) copy-start(bf16[512,512]{1,0:T(8,128)(2,1)} %param.20) | copy-start | bytes 1572868
  48.0 1.0 copy-start.10
  49.0 2.0 copy-start.14
  49.0 2.0 copy-start.18
  51.0 1.7 copy-start.21
  51.0 1.9 copy-start.1
  53.1 3.6 copy-start.5
  78.8 21.9 %copy-start.3 = (bf16[1024,512]{1,0:T(8,128)(2,1)}, bf16[1024,512]{1,0:T(8,128)(2,1)S(1)}, u32[]{:S(2)}) copy-start(bf16[1024,512]{1,0:T(8,128)(2,1)S(1)} %get-tuple-element.19) | copy-start | bytes 3145732
  95.9 1.2 copy-start.15
  97.8 1.2 copy-start.6
  97.8 1.3 copy-start.11
  103.1 1.0 copy-start.20
  103.1 3.1 copy-start.22
  103.1 3.1 copy-start.2
  103.1 269.6 %all-reduce.5.cloned.1.call-start = ((), (), s32[]{:S(2)}) async-start(), calls=%async_computation.1 | async-start | bytes 2572288 | tf_op jit(solution)/shard_map/psum | solution.py:313
  106.2 24.7 %copy-start.9 = (bf16[2048,512]{1,0:T(8,128)(2,1)S(1)}, bf16[2048,512]{1,0:T(8,128)(2,1)}, u32[]{:S(2)}) copy-start(bf16[2048,512]{1,0:T(8,128)(2,1)} %copy-done.8) | copy-start | bytes 6291460
  130.9 2.1 copy-start.13
  139.6 96.7 %copy-start.4 = (bf16[1024,512]{1,0:T(8,128)(2,1)S(1)}, bf16[1024,512]{1,0:T(8,128)(2,1)}, u32[]{:S(2)}) copy-start(bf16[1024,512]{1,0:T(8,128)(2,1)} %copy-done.3) | copy-start | bytes 3145732
  139.6 96.7 %copy-start.16 = (bf16[1024,512]{1,0:T(8,128)(2,1)S(1)}, bf16[1024,512]{1,0:T(8,128)(2,1)}, u32[]{:S(2)}) copy-start(bf16[1024,512]{1,0:T(8,128)(2,1)} %copy-done.14) | copy-start | bytes 3145732
  236.4 2.9 copy-start.7
Sparse Core Ops, SparseCore 0:
  103.2 133.0 all-reduce.2
  242.6 130.0 all-reduce.4
